TPU v7x, 32 devices: a whole 2x2x4 slice. The times are simulated.
32 devices in a mesh: row: 8 (over z, x), col: 4 (over y, core).
Axes of the slice: x: 2, y: 2, z: 4, core: 2. Of those that a mesh axis runs over, the one named last changes fastest.
Arguments:
- volume: float32 [32, 128, 512], P('col', 'row'), may hold values from -4 to 4
Outputs:
- denoised: float32 [32, 128, 512], P('col', 'row')
- flux_x: float32 [32, 128, 512], P('col', 'row')
All inputs are finite; a program needn't handle non-finite values.
Results may differ from a plain program's by a relative error of at most 0.00014.
Values sent between devices are 32-bit elements; how exact they have to be, the bound alone decides.
A program may use at most 64 MiB of HBM per device.

v0:
```python
import functools
import math

import jax
import jax.numpy as jnp
import numpy as np
from jax import lax
from jax.experimental import pallas as pl
from jax.experimental.pallas import tpu as pltpu
from jax.sharding import PartitionSpec as P

PASSES = 3


HIGHEST = lax.Precision.HIGHEST
TIME_STEP = 0.16
EDGE_SCALE = 2.0
LOW_DIFFUSIVITY = 0.2
DIFFUSIVITY_SPAN = 1.8
GRAY_SLOPE = 2.5
REFERENCE_DIFFUSIVITY = 1.1


def with_halo(block, sides, width):
    for axis, dim in sides:
        count = lax.axis_size(axis)
        forward = [(i, i + 1) for i in range(count - 1)]
        forward.append((count - 1, 0))
        backward = [(target, source) for source, target in forward]
        low = lax.ppermute(
            lax.slice_in_dim(block, block.shape[dim] - width, None, axis=dim), axis, forward
        )
        high = lax.ppermute(lax.slice_in_dim(block, 0, width, axis=dim), axis, backward)
        block = jnp.concatenate([low, block, high], axis=dim)
    return block


def diffuse(padded):
    center = padded[1:-1, 1:-1, :]
    summed = jnp.zeros_like(center)
    neighbours = (
        padded[:-2, 1:-1, :],
        padded[2:, 1:-1, :],
        padded[1:-1, :-2, :],
        padded[1:-1, 2:, :],
        jnp.roll(center, 1, axis=2),
        jnp.roll(center, -1, axis=2),
    )
    for member in neighbours:
        differ = member - center
        summed = summed + differ / (1.0 + (differ / EDGE_SCALE) ** 2)
    return center + TIME_STEP * summed


def phase_of(integers, length):
    return (integers % length).astype(jnp.float32) * (2.0 * math.pi / length)


def dft_table(length):
    counter = jnp.arange(length, dtype=jnp.int32)
    angles = phase_of(counter[:, None] * counter[None, :], length)
    return (jnp.cos(angles), jnp.sin(angles))


def plane_table(z_cells, y_cells, along_z):
    counter = jnp.arange(z_cells * y_cells, dtype=jnp.int32)
    z_place = counter // y_cells
    y_place = counter % y_cells
    if along_z:
        same = y_place[:, None] == y_place[None, :]
        angles = phase_of(z_place[:, None] * z_place[None, :], z_cells)
    else:
        same = z_place[:, None] == z_place[None, :]
        angles = phase_of(y_place[:, None] * y_place[None, :], y_cells)
    return (jnp.where(same, jnp.cos(angles), 0.0), jnp.where(same, jnp.sin(angles), 0.0))


def contract(pieces, tables, pattern, orient):
    real_part, imag_part = pieces
    cosine, sine_part = tables
    real_cos = jnp.einsum(pattern, real_part, cosine, precision=HIGHEST)
    imag_sin = jnp.einsum(pattern, imag_part, sine_part, precision=HIGHEST)
    imag_cos = jnp.einsum(pattern, imag_part, cosine, precision=HIGHEST)
    real_sin = jnp.einsum(pattern, real_part, sine_part, precision=HIGHEST)
    return (real_cos - orient * imag_sin, imag_cos + orient * real_sin)


def rotate(pieces, angles, orient):
    cosine = jnp.cos(angles)
    sine_part = jnp.sin(angles)
    real_part, imag_part = pieces
    return (
        real_part * cosine - orient * imag_part * sine_part,
        imag_part * cosine + orient * real_part * sine_part,
    )


def y_twiddle(row_count, z_cells, y_cells):
    within = jnp.arange(z_cells * y_cells, dtype=jnp.int32) % y_cells
    orders = jnp.arange(row_count, dtype=jnp.int32)
    return phase_of(orders[:, None] * within[None, :], row_count * y_cells)[:, None, :]


def z_twiddle(col_count, z_cells, y_cells):
    within = jnp.arange(z_cells * y_cells, dtype=jnp.int32) // y_cells
    orders = jnp.arange(col_count, dtype=jnp.int32)
    return phase_of(orders[:, None] * within[None, :], col_count * z_cells)[:, None, None, :]


def row_transpose(pieces):
    return (
        lax.all_to_all(pieces[0], "row", split_axis=1, concat_axis=1, tiled=True),
        lax.all_to_all(pieces[1], "row", split_axis=1, concat_axis=1, tiled=True),
    )


def col_transpose(pieces):
    return (
        lax.all_to_all(pieces[0], "col", split_axis=1, concat_axis=1, tiled=True),
        lax.all_to_all(pieces[1], "col", split_axis=1, concat_axis=1, tiled=True),
    )


def reshape_all(pieces, extent):
    return (pieces[0].reshape(extent), pieces[1].reshape(extent))


def forward(source):
    fields, z_cells, y_cells, x_cells = source.shape
    row_count = lax.axis_size("row")
    col_count = lax.axis_size("col")
    half_width = x_cells // 2
    per_row = half_width // row_count
    block_share = row_count // col_count
    plane_cells = z_cells * y_cells
    flat = source.reshape(fields, plane_cells, x_cells)
    x_index = jnp.arange(x_cells, dtype=jnp.int32)
    k_index = jnp.arange(half_width, dtype=jnp.int32)
    angles = phase_of(x_index[:, None] * k_index[None, :], x_cells)
    real_part = jnp.einsum("fmx,xk->fkm", flat, jnp.cos(angles), precision=HIGHEST)
    imag_part = -jnp.einsum("fmx,xk->fkm", flat, jnp.sin(angles), precision=HIGHEST)
    pieces = reshape_all((real_part, imag_part), (fields, row_count, per_row, plane_cells))
    pieces = row_transpose(pieces)
    pieces = contract(pieces, dft_table(row_count), "fskm,sp->fpkm", -1.0)
    pieces = rotate(pieces, y_twiddle(row_count, z_cells, y_cells), -1.0)
    pieces = contract(pieces, plane_table(z_cells, y_cells, False), "fpkm,mn->fpkn", -1.0)
    pieces = reshape_all(pieces, (fields, col_count, block_share * per_row * plane_cells))
    pieces = col_transpose(pieces)
    pieces = reshape_all(pieces, (fields, col_count, block_share, per_row, plane_cells))
    pieces = contract(pieces, dft_table(col_count), "fcabm,cp->fpabm", -1.0)
    pieces = rotate(pieces, z_twiddle(col_count, z_cells, y_cells), -1.0)
    return contract(pieces, plane_table(z_cells, y_cells, True), "fpabm,mn->fpabn", -1.0)


def inverse(pieces, z_cells, y_cells, x_cells):
    fields, col_count, block_share, per_row, plane_cells = pieces[0].shape
    row_count = col_count * block_share
    half_width = row_count * per_row
    pieces = contract(pieces, plane_table(z_cells, y_cells, True), "fpabn,nm->fpabm", 1.0)
    pieces = rotate(pieces, z_twiddle(col_count, z_cells, y_cells), 1.0)
    pieces = contract(pieces, dft_table(col_count), "fpabm,pc->fcabm", 1.0)
    pieces = reshape_all(pieces, (fields, col_count, block_share * per_row * plane_cells))
    pieces = col_transpose(pieces)
    pieces = reshape_all(pieces, (fields, row_count, per_row, plane_cells))
    pieces = contract(pieces, plane_table(z_cells, y_cells, False), "fpkn,nm->fpkm", 1.0)
    pieces = rotate(pieces, y_twiddle(row_count, z_cells, y_cells), 1.0)
    pieces = contract(pieces, dft_table(row_count), "fpkm,ps->fskm", 1.0)
    pieces = row_transpose(pieces)
    pieces = reshape_all(pieces, (fields, half_width, plane_cells))
    k_index = jnp.arange(half_width, dtype=jnp.int32)
    x_index = jnp.arange(x_cells, dtype=jnp.int32)
    angles = phase_of(k_index[:, None] * x_index[None, :], x_cells)
    weight = jnp.where(k_index == 0, 1.0, 2.0).astype(jnp.float32)[:, None]
    real_out = jnp.einsum("fkm,kx->fmx", pieces[0], weight * jnp.cos(angles), precision=HIGHEST)
    imag_out = jnp.einsum("fkm,kx->fmx", pieces[1], weight * jnp.sin(angles), precision=HIGHEST)
    return (real_out - imag_out).reshape(fields, z_cells, y_cells, x_cells)


def spectral_tables(z_cells, y_cells, x_cells):
    row_count = lax.axis_size("row")
    col_count = lax.axis_size("col")
    block_share = row_count // col_count
    per_row = x_cells // 2 // row_count
    plane = jnp.arange(z_cells * y_cells, dtype=jnp.int32)
    z_wave = (
        jnp.arange(col_count, dtype=jnp.int32)[:, None, None, None]
        + col_count * (plane // y_cells)[None, None, None, :]
    )
    y_wave = (lax.axis_index("col") * block_share + jnp.arange(block_share, dtype=jnp.int32))[
        None, :, None, None
    ] + row_count * (plane % y_cells)[None, None, None, :]
    x_wave = (lax.axis_index("row") * per_row + jnp.arange(per_row, dtype=jnp.int32))[
        None, None, :, None
    ]
    k_extent = (col_count, block_share, per_row, z_cells * y_cells)
    angle_list = [
        jnp.broadcast_to(member, k_extent)
        for member in (
            phase_of(x_wave, x_cells),
            phase_of(y_wave, row_count * y_cells),
            phase_of(z_wave, col_count * z_cells),
        )
    ]
    plus_symbols = [(jnp.cos(member) - 1.0, jnp.sin(member)) for member in angle_list]
    minus_symbols = [(1.0 - jnp.cos(member), jnp.sin(member)) for member in angle_list]
    spread = (
        4.0 * jnp.sin(0.5 * angle_list[0]) ** 2
        + 4.0 * jnp.sin(0.5 * angle_list[1]) ** 2
        + 4.0 * jnp.sin(0.5 * angle_list[2]) ** 2
    )
    zero_mode = (x_wave == 0) & (y_wave == 0) & (z_wave == 0)
    total_cells = float(x_cells * row_count * y_cells * col_count * z_cells)
    multiplier = jnp.where(
        zero_mode,
        0.0,
        1.0 / (REFERENCE_DIFFUSIVITY * jnp.where(zero_mode, 1.0, spread) * total_cells),
    )
    return (plus_symbols, minus_symbols, multiplier)


def times_symbol(symbol, pieces):
    symbol_real, symbol_imag = symbol
    return (
        symbol_real * pieces[0] - symbol_imag * pieces[1],
        symbol_real * pieces[1] + symbol_imag * pieces[0],
    )


def stack_symbols(symbols, pieces):
    products = [times_symbol(symbol, pieces) for symbol in symbols]
    return (
        jnp.concatenate([member[0] for member in products], axis=0),
        jnp.concatenate([member[1] for member in products], axis=0),
    )


def contract_symbols(symbols, pieces):
    real_sum = jnp.zeros_like(pieces[0][0:1])
    imag_sum = jnp.zeros_like(pieces[1][0:1])
    for direction in range(3):
        product = times_symbol(
            symbols[direction],
            (pieces[0][direction : direction + 1], pieces[1][direction : direction + 1]),
        )
        real_sum = real_sum + product[0]
        imag_sum = imag_sum + product[1]
    return (real_sum, imag_sum)


def rescale(multiplier, pieces):
    return (multiplier * pieces[0], multiplier * pieces[1])


def on_device_general(volume):
    z_cells, y_cells, x_cells = volume.shape
    smooth = volume
    for sweep_index in range(PASSES):
        padded = with_halo(smooth, (("row", 1), ("col", 0)), 1)
        smooth = diffuse(padded)
    diffusivity = LOW_DIFFUSIVITY + DIFFUSIVITY_SPAN * jax.nn.sigmoid(GRAY_SLOPE * smooth)
    excess = diffusivity - REFERENCE_DIFFUSIVITY
    plus_symbols, minus_symbols, multiplier = spectral_tables(z_cells, y_cells, x_cells)
    source = (excess - jnp.roll(excess, 1, axis=2))[None]
    potential_hat = rescale(multiplier, forward(source))
    unit_load = jnp.array([1.0, 0.0, 0.0], jnp.float32)[:, None, None, None]
    gradients = inverse(stack_symbols(plus_symbols, potential_hat), z_cells, y_cells, x_cells)
    tau_hat = forward(excess[None] * (gradients + unit_load))
    potential_hat = rescale(multiplier, contract_symbols(minus_symbols, tau_hat))
    gradient_x = inverse(times_symbol(plus_symbols[0], potential_hat), z_cells, y_cells, x_cells)[0]
    flux_x = diffusivity * (1.0 + gradient_x)
    return (smooth, flux_x)


MESH = pl.DeviceIdType.MESH
NT = (((1,), (1,)), ((), ()))
NN = (((1,), (0,)), ((), ()))
LANES = 128
SUBLANES = 8
EXCHANGES = PASSES + 1


def split(values):
    high = values.astype(jnp.bfloat16)
    return high, (values - high.astype(jnp.float32)).astype(jnp.bfloat16)


def split_numpy(values):
    high = values.astype(np.float32).astype(jnp.bfloat16)
    return high, (values - high.astype(np.float64)).astype(np.float32).astype(jnp.bfloat16)


def host_tables(rows, cols, z_cells, y_cells, x_cells):
    devices = rows * cols
    half = x_cells // 2
    k = np.arange(half)
    turn = 2.0 * np.pi * ((k[:, None] * np.arange(x_cells)[None, :]) % x_cells) / x_cells
    wave = np.stack([np.cos(turn), -np.sin(turn)])
    wave = wave.reshape(2, devices, SUBLANES, x_cells).transpose(1, 0, 2, 3)
    wave = wave.reshape(2 * half, x_cells)
    zl, yl = np.divmod(np.arange(LANES), y_cells)
    c, r = np.divmod(np.arange(devices), rows)
    inner = 2.0 * np.pi * (zl[:, None] * zl[None, :] / z_cells + yl[:, None] * yl[None, :] / y_cells)
    cosine, sine = np.cos(inner), np.sin(inner)
    plane = np.block([[cosine, -sine], [sine, cosine]])
    nz, ny = cols * z_cells, rows * y_cells
    twist = 2.0 * np.pi * (c[:, None] * zl[None, :] / nz + r[:, None] * yl[None, :] / ny)
    kz = c[:, None] + cols * zl[None, :]
    ky = r[:, None] + rows * yl[None, :]
    lam_zy = 4.0 * np.sin(np.pi * kz / nz) ** 2 + 4.0 * np.sin(np.pi * ky / ny) ** 2
    lam_x = (4.0 * np.sin(np.pi * k / x_cells) ** 2).reshape(devices, SUBLANES, 1)
    weight = np.where(k == 0, 1.0, 2.0) / (REFERENCE_DIFFUSIVITY * nz * ny * x_cells)
    weight = weight.reshape(devices, SUBLANES, 1)
    shape = (devices, SUBLANES, LANES)
    small = np.stack(
        [
            np.broadcast_to(np.cos(twist)[:, None, :], shape),
            np.broadcast_to(np.sin(twist)[:, None, :], shape),
            np.broadcast_to(lam_zy[:, None, :], shape),
            np.broadcast_to(lam_x, shape),
            np.broadcast_to(weight, shape),
        ]
    ).astype(np.float32)
    return split_numpy(wave) + split_numpy(plane) + (small,)


def small_fft(items, sign):
    size = len(items)
    if size == 1:
        return items
    even, odd = small_fft(items[::2], sign), small_fft(items[1::2], sign)
    low, high = [], []
    for k in range(size // 2):
        (er, ei), (xr, xi) = even[k], odd[k]
        if 4 * k == size:
            xr, xi = -sign * xi, sign * xr
        elif k:
            co, si = math.cos(2 * math.pi * k / size), sign * math.sin(2 * math.pi * k / size)
            xr, xi = xr * co - xi * si, xr * si + xi * co
        low.append((er + xr, ei + xi))
        high.append((er - xr, ei - xi))
    return low + high


def grid_fft(items, rows, cols, sign):
    lines = [small_fft(items[c * rows : (c + 1) * rows], sign) for c in range(cols)]
    columns = [small_fft([lines[c][r] for c in range(cols)], sign) for r in range(rows)]
    return [columns[r][c] for c in range(cols) for r in range(rows)]


def kernel(
    rows, cols, z_cells, y_cells, x_cells,
    volume, wave_hi_hbm, wave_lo_hbm, plane_hi_hbm, plane_lo_hbm, small_hbm,
    smooth_out, flux_out,
    wave_hi, wave_lo, plane_hi, plane_lo, small,
    field, excess_ref, y_send, y_recv, z_recv, ey_send, ey_recv, ez_recv,
    packed, arrived,
    table_sem, halo_send, halo_recv, e_send, e_recv, all_send, all_recv,
):
    devices = rows * cols
    cells = z_cells * y_cells
    row, col = lax.axis_index("row"), lax.axis_index("col")
    me = col * rows + row
    up_row, down_row = lax.rem(row + 1, rows), lax.rem(row + rows - 1, rows)
    up_col, down_col = lax.rem(col + 1, cols), lax.rem(col + cols - 1, cols)

    loads = [
        pltpu.make_async_copy(source, target, table_sem.at[i])
        for i, (source, target) in enumerate(
            (
                (wave_hi_hbm, wave_hi), (wave_lo_hbm, wave_lo), (plane_hi_hbm, plane_hi),
                (plane_lo_hbm, plane_lo), (small_hbm, small),
            )
        )
    ]
    for load in loads:
        load.start()

    barrier = pltpu.get_barrier_semaphore()

    def greet(step, carry):
        other = lax.rem(me + step, devices)
        pl.semaphore_signal(
            barrier, inc=1, device_id=(lax.rem(other, rows), other // rows), device_id_type=MESH
        )
        return carry

    lax.fori_loop(1, devices, greet, 0)
    pl.semaphore_wait(barrier, devices - 1)

    place = lax.broadcasted_iota(jnp.int32, (cells, x_cells), 0)
    first_y = lax.rem(place, y_cells) == 0
    last_y = lax.rem(place, y_cells) == y_cells - 1

    def spread(edge):
        wide = jnp.broadcast_to(edge[:, None, :], (z_cells, y_cells, x_cells))
        return wide.reshape(cells, x_cells)

    def edge_of(values, y):
        return values.reshape(z_cells, y_cells, x_cells)[:, y, :]

    def remote(source, target, send, recv, device):
        return pltpu.make_async_remote_copy(
            src_ref=source, dst_ref=target, send_sem=send, recv_sem=recv,
            device_id=device, device_id_type=MESH,
        )

    def start_halo(e):
        y_send[e, 0] = edge_of(field[e], y_cells - 1)
        y_send[e, 1] = edge_of(field[e], 0)
        copies = (
            remote(y_send.at[e, 0], y_recv.at[e, 0], halo_send.at[e, 0], halo_recv.at[e, 0], (up_row, col)),
            remote(y_send.at[e, 1], y_recv.at[e, 1], halo_send.at[e, 1], halo_recv.at[e, 1], (down_row, col)),
            remote(field.at[e, pl.ds(cells - y_cells, y_cells)], z_recv.at[e, 0],
                   halo_send.at[e, 2], halo_recv.at[e, 2], (row, up_col)),
            remote(field.at[e, pl.ds(0, y_cells)], z_recv.at[e, 1],
                   halo_send.at[e, 3], halo_recv.at[e, 3], (row, down_col)),
        )
        for copy in copies:
            copy.start()
        return copies

    def next_x(v):
        return pltpu.roll(v, x_cells - 1, 1)

    def prev_x(v):
        return pltpu.roll(v, 1, 1)

    def limited(differ):
        scaled = differ / EDGE_SCALE
        return differ / (1.0 + scaled * scaled)

    pending = []
    field[0] = volume[...].reshape(cells, x_cells)
    for sweep in range(PASSES):
        copies = start_halo(sweep)
        pending += copies
        now = field[sweep]
        flow = limited(next_x(now) - now)
        total = flow - prev_x(flow)
        inner_z = limited(now[y_cells:] - now[:-y_cells])
        for copy in copies:
            copy.wait_recv()
        above = jnp.where(last_y, spread(y_recv[sweep, 1]), pltpu.roll(now, cells - 1, 0))
        flow = limited(above - now)
        edge = limited(edge_of(now, 0) - y_recv[sweep, 0])
        total = total + (flow - jnp.where(first_y, spread(edge), pltpu.roll(flow, 1, 0)))
        z_low = limited(now[:y_cells] - z_recv[sweep, 0])
        z_high = limited(z_recv[sweep, 1] - now[-y_cells:])
        total = total + (
            jnp.concatenate([inner_z, z_high], axis=0) - jnp.concatenate([z_low, inner_z], axis=0)
        )
        later = now + TIME_STEP * total
        if sweep < PASSES - 1:
            field[sweep + 1] = later
    smooth_out[...] = later.reshape(z_cells, y_cells, x_cells)
    diffusivity = LOW_DIFFUSIVITY + DIFFUSIVITY_SPAN / (1.0 + jnp.exp(-GRAY_SLOPE * later))
    flux_out[...] = diffusivity.reshape(z_cells, y_cells, x_cells)
    excess = diffusivity - REFERENCE_DIFFUSIVITY
    excess_ref[...] = excess
    ey_send[...] = edge_of(excess, y_cells - 1)
    e_copies = (
        remote(ey_send, ey_recv, e_send.at[0], e_recv.at[0], (up_row, col)),
        remote(excess_ref.at[pl.ds(cells - y_cells, y_cells)], ez_recv, e_send.at[1], e_recv.at[1], (row, up_col)),
    )
    for copy in e_copies:
        copy.start()
    pending += e_copies
    for load in loads:
        load.wait()

    def exchange(turn):
        def send(step, carry):
            other = lax.rem(me + step, devices)
            remote(
                packed.at[turn, other], arrived.at[turn, me], all_send.at[turn], all_recv.at[turn],
                (lax.rem(other, rows), other // rows),
            ).start()
            return carry

        lax.fori_loop(1, devices, send, 0)
        arrived[turn, me] = packed[turn, me]
        block = arrived.at[turn, pl.ds(0, devices - 1)]
        pltpu.make_async_copy(block, block, all_recv.at[turn]).wait()

    def finish(turn):
        block = packed.at[turn, pl.ds(0, devices - 1)]
        pltpu.make_async_copy(block, block, all_send.at[turn]).wait()

    def product(a, b, dims):
        return lax.dot_general(a, b, dims, preferred_element_type=jnp.float32)

    def row_product(values, high, low, dims):
        values_hi, values_lo = split(values)
        count = values.shape[0]
        both = product(jnp.concatenate([values_hi, values_lo], axis=0), high, dims)
        return both[:count] + (both[count:] + product(values_hi, low, dims))

    def solve(source, turn):
        source_hi, source_lo = split(source)
        both = product(wave_hi[...], jnp.concatenate([source_hi, source_lo], axis=0), NT)
        spectrum = both[:, :cells] + (both[:, cells:] + product(wave_lo[...], source_hi, NT))
        packed[turn] = spectrum.reshape(devices, 2 * SUBLANES, LANES)
        exchange(turn)
        items = [(arrived[turn, d, :SUBLANES], arrived[turn, d, SUBLANES:]) for d in range(devices)]
        items = grid_fft(items, rows, cols, -1.0)
        turned = []
        for d, (re, im) in enumerate(items):
            co, si = small[0, d], small[1, d]
            turned.append(jnp.concatenate([re * co + im * si, im * co - re * si], axis=1))
        waves = row_product(jnp.concatenate(turned, axis=0), plane_hi[...], plane_lo[...], NN)
        lam = small[2] + small[3, me][None]
        factor = jnp.where(lam == 0.0, 0.0, small[4, me][None] / jnp.where(lam == 0.0, 1.0, lam))
        factor = factor.reshape(devices * SUBLANES, LANES)
        waves = waves * jnp.concatenate([factor, factor], axis=1)
        waves = row_product(waves, plane_hi[...], plane_lo[...], NT)
        items = []
        for d in range(devices):
            part = waves[d * SUBLANES : (d + 1) * SUBLANES]
            re, im = part[:, :LANES], part[:, LANES:]
            co, si = small[0, d], small[1, d]
            items.append((re * co - im * si, im * co + re * si))
        items = grid_fft(items, rows, cols, 1.0)
        for d, (re, im) in enumerate(items):
            packed[turn + 1, d, :SUBLANES] = re
            packed[turn + 1, d, SUBLANES:] = im
        exchange(turn + 1)
        back = arrived[turn + 1].reshape(2 * SUBLANES * devices, LANES)
        return row_product(back.T, wave_hi[...], wave_lo[...], NN)

    potential = solve(excess - prev_x(excess), 0)
    field[PASSES] = potential
    copies = start_halo(PASSES)
    pending += copies
    potential = field[PASSES]
    excess = excess_ref[...]
    tau = excess * (1.0 + (next_x(potential) - potential))
    diverge = tau - prev_x(tau)
    inner_z = excess[:-y_cells] * (potential[y_cells:] - potential[:-y_cells])
    for copy in e_copies + copies:
        copy.wait_recv()
    above = jnp.where(last_y, spread(y_recv[PASSES, 1]), pltpu.roll(potential, cells - 1, 0))
    tau = excess * (above - potential)
    edge = ey_recv[...] * (edge_of(potential, 0) - y_recv[PASSES, 0])
    diverge = diverge + (tau - jnp.where(first_y, spread(edge), pltpu.roll(tau, 1, 0)))
    z_low = ez_recv[...] * (potential[:y_cells] - z_recv[PASSES, 0])
    z_high = excess[-y_cells:] * (z_recv[PASSES, 1] - potential[-y_cells:])
    diverge = diverge + (
        jnp.concatenate([inner_z, z_high], axis=0) - jnp.concatenate([z_low, inner_z], axis=0)
    )
    potential = solve(diverge, 2)
    gradient = next_x(potential) - potential
    flux_out[...] = flux_out[...] * (1.0 + gradient.reshape(z_cells, y_cells, x_cells))
    for copy in pending:
        copy.wait_send()
    for turn in range(4):
        finish(turn)


def on_device(rows, cols, tables, volume):
    z_cells, y_cells, x_cells = volume.shape
    devices, cells = rows * cols, z_cells * y_cells
    f32, bf16 = jnp.float32, jnp.bfloat16
    vmem = pl.BlockSpec(memory_space=pltpu.VMEM)
    scratch = [pltpu.VMEM(table.shape, table.dtype) for table in tables] + [
        pltpu.VMEM((EXCHANGES, cells, x_cells), f32),
        pltpu.VMEM((cells, x_cells), f32),
        pltpu.VMEM((EXCHANGES, 2, z_cells, x_cells), f32),
        pltpu.VMEM((EXCHANGES, 2, z_cells, x_cells), f32),
        pltpu.VMEM((EXCHANGES, 2, y_cells, x_cells), f32),
        pltpu.VMEM((z_cells, x_cells), f32),
        pltpu.VMEM((z_cells, x_cells), f32),
        pltpu.VMEM((y_cells, x_cells), f32),
        pltpu.VMEM((4, devices, 2 * SUBLANES, LANES), f32),
        pltpu.VMEM((4, devices, 2 * SUBLANES, LANES), f32),
        pltpu.SemaphoreType.DMA((len(tables),)),
        pltpu.SemaphoreType.DMA((EXCHANGES, 4)),
        pltpu.SemaphoreType.DMA((EXCHANGES, 4)),
        pltpu.SemaphoreType.DMA((2,)),
        pltpu.SemaphoreType.DMA((2,)),
        pltpu.SemaphoreType.DMA((4,)),
        pltpu.SemaphoreType.DMA((4,)),
    ]
    shape = jax.ShapeDtypeStruct(volume.shape, f32)
    return pl.pallas_call(
        functools.partial(kernel, rows, cols, z_cells, y_cells, x_cells),
        out_shape=(shape, shape),
        in_specs=[vmem] + [pl.BlockSpec(memory_space=pl.ANY)] * len(tables),
        out_specs=(vmem, vmem),
        scratch_shapes=scratch,
        compiler_params=pltpu.CompilerParams(
            collective_id=0, has_side_effects=True, vmem_limit_bytes=32 * 1024 * 1024
        ),
    )(volume, *tables)


def power_of_two(count):
    return count & (count - 1) == 0


def block_function(rows, cols, volume):
    z_cells, y_cells, x_cells = volume.shape
    devices = rows * cols
    direct = (
        x_cells // 2 == SUBLANES * devices
        and z_cells * y_cells == LANES
        and z_cells % 8 == 0
        and y_cells % 8 == 0
        and power_of_two(rows)
        and power_of_two(cols)
        and min(rows, cols) > 2
    )
    if not direct:
        return on_device_general(volume)
    tables = [jnp.asarray(t) for t in host_tables(rows, cols, z_cells, y_cells, x_cells)]
    return on_device(rows, cols, tables, volume)


def solution(mesh):
    return jax.shard_map(
        functools.partial(block_function, mesh.shape["row"], mesh.shape["col"]),
        mesh=mesh,
        in_specs=(P("col", "row", None),),
        out_specs=(P("col", "row", None), P("col", "row", None)),
        check_vma=False,
    )
```

profile of v0, /device:TPU:0, one launch (start us, length us, event | category | flops | bytes accessed | tf_op | source)
XLA Modules:
  0.0 65.2 jit_solution(12040438130059295449)
XLA Ops:
  0.6 0.0 copy-start
  0.6 1.1 %copy-done = f32[5,32,8,128]{3,2,1,0:T(8,128)S(1)} copy-done((f32[5,32,8,128]{3,2,1,0:T(8,128)S(1)}, f32[5,32,8,128]{3,2,1,0:T(8,128)}, u32[]{:S(2)}) %copy-start) | copy-done | bytes 655384
  1.7 0.0 copy-start.1
  1.7 1.0 %copy-done.1 = bf16[512,512]{1,0:T(8,128)(2,1)S(1)} copy-done((bf16[512,512]{1,0:T(8,128)(2,1)S(1)}, bf16[512,512]{1,0:T(8,128)(2,1)}, u32[]{:S(2)}) %copy-start.1) | copy-done | bytes 524312
  2.8 0.0 copy-start.2
  2.8 1.0 %copy-done.2 = bf16[512,512]{1,0:T(8,128)(2,1)S(1)} copy-done((bf16[512,512]{1,0:T(8,128)(2,1)S(1)}, bf16[512,512]{1,0:T(8,128)(2,1)}, u32[]{:S(2)}) %copy-start.2) | copy-done | bytes 524312
  3.8 0.0 copy-start.3
  3.8 0.9 %copy-done.3 = f32[8,16,512]{2,1,0:T(8,128)S(1)} copy-done((f32[8,16,512]{2,1,0:T(8,128)S(1)}, f32[8,16,512]{2,1,0:T(8,128)}, u32[]{:S(2)}) %copy-start.3) | copy-done | bytes 262168
  4.8 0.0 copy-start.4
  4.8 0.9 %copy-done.4 = bf16[256,256]{1,0:T(8,128)(2,1)S(1)} copy-done((bf16[256,256]{1,0:T(8,128)(2,1)S(1)}, bf16[256,256]{1,0:T(8,128)(2,1)}, u32[]{:S(2)}) %copy-start.4) | copy-done | bytes 131096
  5.7 0.0 copy-start.5
  5.7 0.9 %copy-done.5 = bf16[256,256]{1,0:T(8,128)(2,1)S(1)} copy-done((bf16[256,256]{1,0:T(8,128)(2,1)S(1)}, bf16[256,256]{1,0:T(8,128)(2,1)}, u32[]{:S(2)}) %copy-start.5) | copy-done | bytes 131096
  6.6 57.2 %shard_map.77 = (f32[8,16,512]{2,1,0:T(8,128)S(1)}, f32[8,16,512]{2,1,0:T(8,128)S(1)}) custom-call(f32[8,16,512]{2,1,0:T(8,128)S(1)} %copy-done.3, bf16[512,512]{1,0:T(8,128)(2,1)S(1)} %copy-done.2, bf16[512,512]{1,0:T(8,128)(2,1)S(1)} %copy-done.1, bf16[256,256]{1,0:T(8,128)(2,1)S(1)} %copy-done.5, bf16[256,256]{1,0:T(8,128)(2,1)S(1)} %copy-done.4, ...), custom_call_target="tpu_custom_call" | custom-call | tf_op jit(solution)/shard_map/pallas_call | solution.py:584
  63.8 0.7 %copy.10 = f32[8,16,512]{2,1,0:T(8,128)} copy(f32[8,16,512]{2,1,0:T(8,128)S(1)} %get-tuple-element.4) | data formatting | bytes 524288
  64.5 0.7 %copy.11 = f32[8,16,512]{2,1,0:T(8,128)} copy(f32[8,16,512]{2,1,0:T(8,128)S(1)} %get-tuple-element.5) | data formatting | bytes 524288
Async XLA Ops:
  0.6 1.1 %copy-start = (f32[5,32,8,128]{3,2,1,0:T(8,128)S(1)}, f32[5,32,8,128]{3,2,1,0:T(8,128)}, u32[]{:S(2)}) copy-start(f32[5,32,8,128]{3,2,1,0:T(8,128)} %constant.14.clone.small_hbm) | copy-start | bytes 1966084
  1.7 1.0 %copy-start.1 = (bf16[512,512]{1,0:T(8,128)(2,1)S(1)}, bf16[512,512]{1,0:T(8,128)(2,1)}, u32[]{:S(2)}) copy-start(bf16[512,512]{1,0:T(8,128)(2,1)} %constant.11.clone.wave_lo_hbm) | copy-start | bytes 1572868
  2.8 1.0 %copy-start.2 = (bf16[512,512]{1,0:T(8,128)(2,1)S(1)}, bf16[512,512]{1,0:T(8,128)(2,1)}, u32[]{:S(2)}) copy-start(bf16[512,512]{1,0:T(8,128)(2,1)} %constant.10.clone.wave_hi_hbm) | copy-start | bytes 1572868
  3.8 0.9 %copy-start.3 = (f32[8,16,512]{2,1,0:T(8,128)S(1)}, f32[8,16,512]{2,1,0:T(8,128)}, u32[]{:S(2)}) copy-start(f32[8,16,512]{2,1,0:T(8,128)} %volume.1) | copy-start | bytes 786436
  4.8 0.9 %copy-start.4 = (bf16[256,256]{1,0:T(8,128)(2,1)S(1)}, bf16[256,256]{1,0:T(8,128)(2,1)}, u32[]{:S(2)}) copy-start(bf16[256,256]{1,0:T(8,128)(2,1)} %constant.13.clone.plane_lo_hbm) | copy-start | bytes 393220
  5.7 0.9 %copy-start.5 = (bf16[256,256]{1,0:T(8,128)(2,1)S(1)}, bf16[256,256]{1,0:T(8,128)(2,1)}, u32[]{:S(2)}) copy-start(bf16[256,256]{1,0:T(8,128)(2,1)} %constant.12.clone.plane_hi_hbm) | copy-start | bytes 393220
where the time goes:
time: 65.5 us; the launch traced here: 65.2 us
  Pallas kernels  57.2 us (87%)
  local copies, waits for them, and re-layouts  7.33 us (11%)
    pallas_call x1, Pallas kernels, on_device(): pl.pallas_call(functools.partial(kernel, rows, cols, z_cells, y_cells, x_...  57.2 us
    unnamed x14, local copies, waits for them, and re-layouts  7.33 us

commit v1 on v0

--- a/solution.py
+++ b/solution.py
@@ -368,7 +368,7 @@
         for i, (source, target) in enumerate(
             (
                 (wave_hi_hbm, wave_hi), (wave_lo_hbm, wave_lo), (plane_hi_hbm, plane_hi),
-                (plane_lo_hbm, plane_lo), (small_hbm, small),
+                (plane_lo_hbm, plane_lo), (small_hbm, small), (volume, field.at[0]),
             )
         )
     ]
@@ -430,7 +430,7 @@
         return differ / (1.0 + scaled * scaled)
 
     pending = []
-    field[0] = volume[...].reshape(cells, x_cells)
+    loads.pop().wait()
     for sweep in range(PASSES):
         copies = start_halo(sweep)
         pending += copies
@@ -470,7 +470,7 @@
 
     def exchange(turn):
         def send(step, carry):
-            other = lax.rem(me + step, devices)
+            other = lax.rem(col + step, cols) * rows + lax.rem(row + step // cols, rows)
             remote(
                 packed.at[turn, other], arrived.at[turn, me], all_send.at[turn], all_recv.at[turn],
                 (lax.rem(other, rows), other // rows),
@@ -572,7 +572,7 @@
         pltpu.VMEM((y_cells, x_cells), f32),
         pltpu.VMEM((4, devices, 2 * SUBLANES, LANES), f32),
         pltpu.VMEM((4, devices, 2 * SUBLANES, LANES), f32),
-        pltpu.SemaphoreType.DMA((len(tables),)),
+        pltpu.SemaphoreType.DMA((len(tables) + 1,)),
         pltpu.SemaphoreType.DMA((EXCHANGES, 4)),
         pltpu.SemaphoreType.DMA((EXCHANGES, 4)),
         pltpu.SemaphoreType.DMA((2,)),
@@ -584,13 +584,13 @@
     return pl.pallas_call(
         functools.partial(kernel, rows, cols, z_cells, y_cells, x_cells),
         out_shape=(shape, shape),
-        in_specs=[vmem] + [pl.BlockSpec(memory_space=pl.ANY)] * len(tables),
+        in_specs=[pl.BlockSpec(memory_space=pl.ANY)] * (len(tables) + 1),
         out_specs=(vmem, vmem),
         scratch_shapes=scratch,
         compiler_params=pltpu.CompilerParams(
-            collective_id=0, has_side_effects=True, vmem_limit_bytes=32 * 1024 * 1024
+            collective_id=0, has_side_effects=True, vmem_limit_bytes=60 * 1024 * 1024
         ),
-    )(volume, *tables)
+    )(volume.reshape(cells, x_cells), *tables)
 
 
 def power_of_two(count):

time: 65.5 us -> 59.5 us (0.908)
  local copies, waits for them, and re-layouts: 7.33 us -> 2.42 us
  Pallas kernels: 57.2 us -> 56.3 us
    unnamed x14 -> x4, local copies, waits for them, and re-layouts: 7.33 us -> 2.42 us
    pallas_call x1, Pallas kernels: 57.2 us -> 56.3 us  [on_device(): pl.pallas_call(functools.partial(kernel, rows, cols, z_cells, y_cells, x_...]
where the time goes in v1:
time: 59.5 us; the launch traced here: 59.3 us
  Pallas kernels  56.3 us (95%)
  local copies, waits for them, and re-layouts  2.42 us (4%)
  between operations  0.65 us (1%)
    pallas_call x1, Pallas kernels, on_device(): pl.pallas_call(functools.partial(kernel, rows, cols, z_cells, y_cells, x_...  56.3 us
    unnamed x4, local copies, waits for them, and re-layouts  2.42 us

profile of v1, /device:TPU:0, one launch (start us, length us, event | category | flops | bytes accessed | tf_op | source)
XLA Modules:
  0.0 59.3 jit_solution(7324494897174587702)
XLA Ops:
  0.6 56.3 %shard_map.77 = (f32[8,16,512]{2,1,0:T(8,128)}, f32[8,16,512]{2,1,0:T(8,128)}) custom-call(f32[128,512]{1,0:T(8,128)} %bitcast.1, bf16[512,512]{1,0:T(8,128)(2,1)} %constant.10.clone.wave_hi_hbm, bf16[512,512]{1,0:T(8,128)(2,1)} %constant.11.clone.wave_lo_hbm, bf16[256,256]{1,0:T(8,128)(2,1)} %constant.12.clone.plane_hi_hbm, ...), custom_call_target="tpu_custom_call" | custom-call | tf_op jit(solution)/shard_map/pallas_call | solution.py:584
  56.9 0.0 copy-start
  56.9 1.7 %copy.10 = f32[8,16,512]{2,1,0:T(8,128)} copy(f32[8,16,512]{2,1,0:T(8,128)} %get-tuple-element.4) | data formatting | bytes 524288
  58.6 0.0 copy-done
  58.6 0.7 %copy.11 = f32[8,16,512]{2,1,0:T(8,128)} copy(f32[8,16,512]{2,1,0:T(8,128)S(1)} %copy-done) | data formatting | bytes 524288
Async XLA Ops:
  56.9 1.7 %copy-start = (f32[8,16,512]{2,1,0:T(8,128)S(1)}, f32[8,16,512]{2,1,0:T(8,128)}, u32[]{:S(2)}) copy-start(f32[8,16,512]{2,1,0:T(8,128)} %get-tuple-element.5) | copy-start | bytes 786436

commit v2 on v1

--- a/solution.py
+++ b/solution.py
@@ -276,6 +276,8 @@
 NN = (((1,), (0,)), ((), ()))
 LANES = 128
 SUBLANES = 8
+HALVES = 2
+QUADS = 4
 EXCHANGES = PASSES + 1
 
 
@@ -291,59 +293,57 @@
 
 def host_tables(rows, cols, z_cells, y_cells, x_cells):
     devices = rows * cols
-    half = x_cells // 2
-    k = np.arange(half)
+    waves = x_cells // 2
+    k = np.arange(waves)
     turn = 2.0 * np.pi * ((k[:, None] * np.arange(x_cells)[None, :]) % x_cells) / x_cells
     wave = np.stack([np.cos(turn), -np.sin(turn)])
-    wave = wave.reshape(2, devices, SUBLANES, x_cells).transpose(1, 0, 2, 3)
-    wave = wave.reshape(2 * half, x_cells)
+    wave = wave.reshape(2, devices, HALVES, QUADS, x_cells).transpose(2, 1, 0, 3, 4)
+    wave = wave.reshape(2 * waves, x_cells)
     zl, yl = np.divmod(np.arange(LANES), y_cells)
     c, r = np.divmod(np.arange(devices), rows)
     inner = 2.0 * np.pi * (zl[:, None] * zl[None, :] / z_cells + yl[:, None] * yl[None, :] / y_cells)
     cosine, sine = np.cos(inner), np.sin(inner)
-    plane = np.block([[cosine, -sine], [sine, cosine]])
+    plane = np.concatenate([cosine, sine], axis=1)
     nz, ny = cols * z_cells, rows * y_cells
     twist = 2.0 * np.pi * (c[:, None] * zl[None, :] / nz + r[:, None] * yl[None, :] / ny)
     kz = c[:, None] + cols * zl[None, :]
     ky = r[:, None] + rows * yl[None, :]
     lam_zy = 4.0 * np.sin(np.pi * kz / nz) ** 2 + 4.0 * np.sin(np.pi * ky / ny) ** 2
-    lam_x = (4.0 * np.sin(np.pi * k / x_cells) ** 2).reshape(devices, SUBLANES, 1)
+    lam_x = 4.0 * np.sin(np.pi * k / x_cells) ** 2
     weight = np.where(k == 0, 1.0, 2.0) / (REFERENCE_DIFFUSIVITY * nz * ny * x_cells)
-    weight = weight.reshape(devices, SUBLANES, 1)
     shape = (devices, SUBLANES, LANES)
-    small = np.stack(
-        [
-            np.broadcast_to(np.cos(twist)[:, None, :], shape),
-            np.broadcast_to(np.sin(twist)[:, None, :], shape),
-            np.broadcast_to(lam_zy[:, None, :], shape),
-            np.broadcast_to(lam_x, shape),
-            np.broadcast_to(weight, shape),
-        ]
-    ).astype(np.float32)
+    sign = np.where(np.arange(SUBLANES) < QUADS, 1.0, -1.0)[None, :, None]
+    members = [np.cos(twist)[:, None, :], np.sin(twist)[:, None, :] * sign, lam_zy[:, None, :]]
+    for member in (lam_x, weight):
+        member = member.reshape(devices, HALVES, 1, QUADS)
+        member = np.broadcast_to(member, (devices, HALVES, 2, QUADS))
+        for half in range(HALVES):
+            members.append(member[:, half].reshape(devices, SUBLANES, 1))
+    small = np.stack([np.broadcast_to(m, shape) for m in members]).astype(np.float32)
     return split_numpy(wave) + split_numpy(plane) + (small,)
 
 
-def small_fft(items, sign):
+def small_fft(items, sign, turned):
     size = len(items)
     if size == 1:
         return items
-    even, odd = small_fft(items[::2], sign), small_fft(items[1::2], sign)
+    even, odd = small_fft(items[::2], sign, turned), small_fft(items[1::2], sign, turned)
     low, high = [], []
     for k in range(size // 2):
-        (er, ei), (xr, xi) = even[k], odd[k]
+        item = odd[k]
         if 4 * k == size:
-            xr, xi = -sign * xi, sign * xr
+            item = -sign * turned(item)
         elif k:
-            co, si = math.cos(2 * math.pi * k / size), sign * math.sin(2 * math.pi * k / size)
-            xr, xi = xr * co - xi * si, xr * si + xi * co
-        low.append((er + xr, ei + xi))
-        high.append((er - xr, ei - xi))
+            angle = 2 * math.pi * k / size
+            item = math.cos(angle) * item - (sign * math.sin(angle)) * turned(item)
+        low.append(even[k] + item)
+        high.append(even[k] - item)
     return low + high
 
 
-def grid_fft(items, rows, cols, sign):
-    lines = [small_fft(items[c * rows : (c + 1) * rows], sign) for c in range(cols)]
-    columns = [small_fft([lines[c][r] for c in range(cols)], sign) for r in range(rows)]
+def grid_fft(items, rows, cols, sign, turned):
+    lines = [small_fft(items[c * rows : (c + 1) * rows], sign, turned) for c in range(cols)]
+    columns = [small_fft([lines[c][r] for c in range(cols)], sign, turned) for r in range(rows)]
     return [columns[r][c] for c in range(cols) for r in range(rows)]
 
 
@@ -468,23 +468,35 @@
     for load in loads:
         load.wait()
 
-    def exchange(turn):
+    def start_exchange(turn, half):
         def send(step, carry):
-            other = lax.rem(col + step, cols) * rows + lax.rem(row + step // cols, rows)
+            to_row = lax.rem(row + step // cols, rows)
+            to_col = lax.rem(col + step, cols)
             remote(
-                packed.at[turn, other], arrived.at[turn, me], all_send.at[turn], all_recv.at[turn],
-                (lax.rem(other, rows), other // rows),
+                packed.at[turn, half, to_col * rows + to_row], arrived.at[turn, half, me],
+                all_send.at[turn, half], all_recv.at[turn, half], (to_row, to_col),
             ).start()
             return carry
 
         lax.fori_loop(1, devices, send, 0)
-        arrived[turn, me] = packed[turn, me]
-        block = arrived.at[turn, pl.ds(0, devices - 1)]
-        pltpu.make_async_copy(block, block, all_recv.at[turn]).wait()
-
-    def finish(turn):
-        block = packed.at[turn, pl.ds(0, devices - 1)]
-        pltpu.make_async_copy(block, block, all_send.at[turn]).wait()
+        arrived[turn, half, me] = packed[turn, half, me]
+
+    def end_exchange(turn, half):
+        block = arrived.at[turn, half, pl.ds(0, devices - 1)]
+        pltpu.make_async_copy(block, block, all_recv.at[turn, half]).wait()
+
+    def finish(turn, half):
+        block = packed.at[turn, half, pl.ds(0, devices - 1)]
+        pltpu.make_async_copy(block, block, all_send.at[turn, half]).wait()
+
+    real_rows = lax.broadcasted_iota(jnp.int32, (SUBLANES, LANES), 0) < QUADS
+
+    def swapped(tile):
+        return pltpu.roll(tile, QUADS, 0)
+
+    def turned(tile):
+        tile = swapped(tile)
+        return jnp.where(real_rows, tile, -tile)
 
     def product(a, b, dims):
         return lax.dot_general(a, b, dims, preferred_element_type=jnp.float32)
@@ -495,37 +507,52 @@
         both = product(jnp.concatenate([values_hi, values_lo], axis=0), high, dims)
         return both[:count] + (both[count:] + product(values_hi, low, dims))
 
+    many = devices * SUBLANES
+    side = lax.rem(lax.broadcasted_iota(jnp.int32, (many, LANES), 0), SUBLANES) < QUADS
+
+    def plane_product(values, sign):
+        both = row_product(values, plane_hi[...], plane_lo[...], NN)
+        cosine, sine = both[:, :LANES], both[:, LANES:]
+        sine = jnp.where(side, pltpu.roll(sine, many - QUADS, 0), -pltpu.roll(sine, QUADS, 0))
+        return cosine - sign * sine
+
+    def spectral(turn, half):
+        items = [arrived[turn, half, d] for d in range(devices)]
+        items = grid_fft(items, rows, cols, -1.0, turned)
+        items = [t * small[0, d] + swapped(t) * small[1, d] for d, t in enumerate(items)]
+        waves = plane_product(jnp.concatenate(items, axis=0), -1.0)
+        lam = small[2] + small[3 + half, me][None]
+        weight = small[3 + HALVES + half, me][None]
+        factor = jnp.where(lam == 0.0, 0.0, weight / jnp.where(lam == 0.0, 1.0, lam))
+        waves = plane_product(waves * factor.reshape(many, LANES), 1.0)
+        items = [waves[d * SUBLANES : (d + 1) * SUBLANES] for d in range(devices)]
+        items = [t * small[0, d] - swapped(t) * small[1, d] for d, t in enumerate(items)]
+        for d, t in enumerate(grid_fft(items, rows, cols, 1.0, turned)):
+            packed[turn + 1, half, d] = t
+
     def solve(source, turn):
         source_hi, source_lo = split(source)
-        both = product(wave_hi[...], jnp.concatenate([source_hi, source_lo], axis=0), NT)
-        spectrum = both[:, :cells] + (both[:, cells:] + product(wave_lo[...], source_hi, NT))
-        packed[turn] = spectrum.reshape(devices, 2 * SUBLANES, LANES)
-        exchange(turn)
-        items = [(arrived[turn, d, :SUBLANES], arrived[turn, d, SUBLANES:]) for d in range(devices)]
-        items = grid_fft(items, rows, cols, -1.0)
-        turned = []
-        for d, (re, im) in enumerate(items):
-            co, si = small[0, d], small[1, d]
-            turned.append(jnp.concatenate([re * co + im * si, im * co - re * si], axis=1))
-        waves = row_product(jnp.concatenate(turned, axis=0), plane_hi[...], plane_lo[...], NN)
-        lam = small[2] + small[3, me][None]
-        factor = jnp.where(lam == 0.0, 0.0, small[4, me][None] / jnp.where(lam == 0.0, 1.0, lam))
-        factor = factor.reshape(devices * SUBLANES, LANES)
-        waves = waves * jnp.concatenate([factor, factor], axis=1)
-        waves = row_product(waves, plane_hi[...], plane_lo[...], NT)
-        items = []
-        for d in range(devices):
-            part = waves[d * SUBLANES : (d + 1) * SUBLANES]
-            re, im = part[:, :LANES], part[:, LANES:]
-            co, si = small[0, d], small[1, d]
-            items.append((re * co - im * si, im * co + re * si))
-        items = grid_fft(items, rows, cols, 1.0)
-        for d, (re, im) in enumerate(items):
-            packed[turn + 1, d, :SUBLANES] = re
-            packed[turn + 1, d, SUBLANES:] = im
-        exchange(turn + 1)
-        back = arrived[turn + 1].reshape(2 * SUBLANES * devices, LANES)
-        return row_product(back.T, wave_hi[...], wave_lo[...], NN)
+        sources = jnp.concatenate([source_hi, source_lo], axis=0)
+        for half in range(HALVES):
+            part = pl.ds(half * many, many)
+            both = product(wave_hi[part, :], sources, NT)
+            spectrum = both[:, :cells] + (
+                both[:, cells:] + product(wave_lo[part, :], source_hi, NT)
+            )
+            packed[turn, half] = spectrum.reshape(devices, SUBLANES, LANES)
+            start_exchange(turn, half)
+        for half in range(HALVES):
+            end_exchange(turn, half)
+            spectral(turn, half)
+            start_exchange(turn + 1, half)
+        total = None
+        for half in range(HALVES):
+            part = pl.ds(half * many, many)
+            end_exchange(turn + 1, half)
+            back = arrived[turn + 1, half].reshape(many, LANES)
+            piece = row_product(back.T, wave_hi[part, :], wave_lo[part, :], NN)
+            total = piece if half == 0 else total + piece
+        return total
 
     potential = solve(excess - prev_x(excess), 0)
     field[PASSES] = potential
@@ -553,7 +580,8 @@
     for copy in pending:
         copy.wait_send()
     for turn in range(4):
-        finish(turn)
+        for half in range(HALVES):
+            finish(turn, half)
 
 
 def on_device(rows, cols, tables, volume):
@@ -570,15 +598,15 @@
         pltpu.VMEM((z_cells, x_cells), f32),
         pltpu.VMEM((z_cells, x_cells), f32),
         pltpu.VMEM((y_cells, x_cells), f32),
-        pltpu.VMEM((4, devices, 2 * SUBLANES, LANES), f32),
-        pltpu.VMEM((4, devices, 2 * SUBLANES, LANES), f32),
+        pltpu.VMEM((4, HALVES, devices, SUBLANES, LANES), f32),
+        pltpu.VMEM((4, HALVES, devices, SUBLANES, LANES), f32),
         pltpu.SemaphoreType.DMA((len(tables) + 1,)),
         pltpu.SemaphoreType.DMA((EXCHANGES, 4)),
         pltpu.SemaphoreType.DMA((EXCHANGES, 4)),
         pltpu.SemaphoreType.DMA((2,)),
         pltpu.SemaphoreType.DMA((2,)),
-        pltpu.SemaphoreType.DMA((4,)),
-        pltpu.SemaphoreType.DMA((4,)),
+        pltpu.SemaphoreType.DMA((4, HALVES)),
+        pltpu.SemaphoreType.DMA((4, HALVES)),
     ]
     shape = jax.ShapeDtypeStruct(volume.shape, f32)
     return pl.pallas_call(

time: 59.5 us -> 58.8 us (0.988)
  Pallas kernels: 56.3 us -> 55.6 us
    pallas_call x1, Pallas kernels: 56.3 us -> 55.6 us  [on_device(): pl.pallas_call(functools.partial(kernel, rows, cols, z_cells, y_cells, x_...]
where the time goes in v2:
time: 58.8 us; the launch traced here: 58.7 us
  Pallas kernels  55.6 us (95%)
  local copies, waits for them, and re-layouts  2.42 us (4%)
  between operations  0.65 us (1%)
    pallas_call x1, Pallas kernels, on_device(): pl.pallas_call(functools.partial(kernel, rows, cols, z_cells, y_cells, x_...  55.6 us
    unnamed x4, local copies, waits for them, and re-layouts  2.42 us

profile of v2, /device:TPU:0, one launch (start us, length us, event | category | flops | bytes accessed | tf_op | source)
XLA Modules:
  0.0 58.7 jit_solution(2695592410807100442)
XLA Ops:
  0.6 55.6 %shard_map.77 = (f32[8,16,512]{2,1,0:T(8,128)}, f32[8,16,512]{2,1,0:T(8,128)}) custom-call(f32[128,512]{1,0:T(8,128)} %bitcast.1, bf16[512,512]{1,0:T(8,128)(2,1)} %constant.10.clone.wave_hi_hbm, bf16[512,512]{1,0:T(8,128)(2,1)} %constant.11.clone.wave_lo_hbm, bf16[128,256]{1,0:T(8,128)(2,1)} %constant.12.clone.plane_hi_hbm, ...), custom_call_target="tpu_custom_call" | custom-call | tf_op jit(solution)/shard_map/pallas_call | solution.py:612
  56.2 0.0 copy-start
  56.2 1.7 %copy.10 = f32[8,16,512]{2,1,0:T(8,128)} copy(f32[8,16,512]{2,1,0:T(8,128)} %get-tuple-element.4) | data formatting | bytes 524288
  58.0 0.0 copy-done
  58.0 0.7 %copy.11 = f32[8,16,512]{2,1,0:T(8,128)} copy(f32[8,16,512]{2,1,0:T(8,128)S(1)} %copy-done) | data formatting | bytes 524288
Async XLA Ops:
  56.2 1.7 %copy-start = (f32[8,16,512]{2,1,0:T(8,128)S(1)}, f32[8,16,512]{2,1,0:T(8,128)}, u32[]{:S(2)}) copy-start(f32[8,16,512]{2,1,0:T(8,128)} %get-tuple-element.5) | copy-start | bytes 786436

commit v3 on v2

--- a/solution.py
+++ b/solution.py
@@ -429,6 +429,17 @@
         scaled = differ / EDGE_SCALE
         return differ / (1.0 + scaled * scaled)
 
+    def between(flow):
+        none = jnp.zeros((y_cells, x_cells), jnp.float32)
+        return jnp.concatenate([flow, none], axis=0) - jnp.concatenate([none, flow], axis=0)
+
+    def z_ends(low, high):
+        none = jnp.zeros((cells - 2 * y_cells, x_cells), jnp.float32)
+        return jnp.concatenate([-low, none, high], axis=0)
+
+    def y_ends(low, high):
+        return jnp.where(last_y, spread(high), jnp.where(first_y, -spread(low), 0.0))
+
     pending = []
     loads.pop().wait()
     for sweep in range(PASSES):
@@ -437,18 +448,20 @@
         now = field[sweep]
         flow = limited(next_x(now) - now)
         total = flow - prev_x(flow)
-        inner_z = limited(now[y_cells:] - now[:-y_cells])
-        for copy in copies:
-            copy.wait_recv()
-        above = jnp.where(last_y, spread(y_recv[sweep, 1]), pltpu.roll(now, cells - 1, 0))
-        flow = limited(above - now)
-        edge = limited(edge_of(now, 0) - y_recv[sweep, 0])
-        total = total + (flow - jnp.where(first_y, spread(edge), pltpu.roll(flow, 1, 0)))
+        flow = jnp.where(last_y, 0.0, limited(pltpu.roll(now, cells - 1, 0) - now))
+        total = total + (flow - pltpu.roll(flow, 1, 0))
+        flow = limited(now[y_cells:] - now[:-y_cells])
+        total = total + between(flow)
+        copies[2].wait_recv()
+        copies[3].wait_recv()
         z_low = limited(now[:y_cells] - z_recv[sweep, 0])
         z_high = limited(z_recv[sweep, 1] - now[-y_cells:])
-        total = total + (
-            jnp.concatenate([inner_z, z_high], axis=0) - jnp.concatenate([z_low, inner_z], axis=0)
-        )
+        total = total + z_ends(z_low, z_high)
+        copies[0].wait_recv()
+        copies[1].wait_recv()
+        y_low = limited(edge_of(now, 0) - y_recv[sweep, 0])
+        y_high = limited(y_recv[sweep, 1] - edge_of(now, y_cells - 1))
+        total = total + y_ends(y_low, y_high)
         later = now + TIME_STEP * total
         if sweep < PASSES - 1:
             field[sweep + 1] = later
@@ -562,18 +575,21 @@
     excess = excess_ref[...]
     tau = excess * (1.0 + (next_x(potential) - potential))
     diverge = tau - prev_x(tau)
-    inner_z = excess[:-y_cells] * (potential[y_cells:] - potential[:-y_cells])
-    for copy in e_copies + copies:
+    tau = excess * jnp.where(last_y, 0.0, pltpu.roll(potential, cells - 1, 0) - potential)
+    diverge = diverge + (tau - pltpu.roll(tau, 1, 0))
+    diverge = diverge + between(excess[:-y_cells] * (potential[y_cells:] - potential[:-y_cells]))
+    for copy in e_copies + copies[2:]:
         copy.wait_recv()
-    above = jnp.where(last_y, spread(y_recv[PASSES, 1]), pltpu.roll(potential, cells - 1, 0))
-    tau = excess * (above - potential)
-    edge = ey_recv[...] * (edge_of(potential, 0) - y_recv[PASSES, 0])
-    diverge = diverge + (tau - jnp.where(first_y, spread(edge), pltpu.roll(tau, 1, 0)))
     z_low = ez_recv[...] * (potential[:y_cells] - z_recv[PASSES, 0])
     z_high = excess[-y_cells:] * (z_recv[PASSES, 1] - potential[-y_cells:])
-    diverge = diverge + (
-        jnp.concatenate([inner_z, z_high], axis=0) - jnp.concatenate([z_low, inner_z], axis=0)
-    )
+    diverge = diverge + z_ends(z_low, z_high)
+    for copy in copies[:2]:
+        copy.wait_recv()
+    y_low = ey_recv[...] * (edge_of(potential, 0) - y_recv[PASSES, 0])
+    y_high = edge_of(excess, y_cells - 1) * (
+        y_recv[PASSES, 1] - edge_of(potential, y_cells - 1)
+    )
+    diverge = diverge + y_ends(y_low, y_high)
     potential = solve(diverge, 2)
     gradient = next_x(potential) - potential
     flux_out[...] = flux_out[...] * (1.0 + gradient.reshape(z_cells, y_cells, x_cells))

time: 58.8 us -> 58.2 us (0.990)
  Pallas kernels: 55.6 us -> 54.9 us
    pallas_call x1, Pallas kernels: 55.6 us -> 54.9 us  [on_device(): pl.pallas_call(functools.partial(kernel, rows, cols, z_cells, y_cells, x_...]
where the time goes in v3:
time: 58.2 us; the launch traced here: 58 us
  Pallas kernels  54.9 us (94%)
  local copies, waits for them, and re-layouts  2.42 us (4%)
  between operations  0.65 us (1%)
    pallas_call x1, Pallas kernels, on_device(): pl.pallas_call(functools.partial(kernel, rows, cols, z_cells, y_cells, x_...  54.9 us
    unnamed x4, local copies, waits for them, and re-layouts  2.42 us

profile of v3, /device:TPU:0, one launch (start us, length us, event | category | flops | bytes accessed | tf_op | source)
XLA Modules:
  0.0 58.0 jit_solution(895169850290579339)
XLA Ops:
  0.6 54.9 %shard_map.77 = (f32[8,16,512]{2,1,0:T(8,128)}, f32[8,16,512]{2,1,0:T(8,128)}) custom-call(f32[128,512]{1,0:T(8,128)} %bitcast.1, bf16[512,512]{1,0:T(8,128)(2,1)} %constant.10.clone.wave_hi_hbm, bf16[512,512]{1,0:T(8,128)(2,1)} %constant.11.clone.wave_lo_hbm, bf16[128,256]{1,0:T(8,128)(2,1)} %constant.12.clone.plane_hi_hbm, ...), custom_call_target="tpu_custom_call" | custom-call | tf_op jit(solution)/shard_map/pallas_call | solution.py:628
  55.6 0.0 copy-start
  55.6 1.7 %copy.10 = f32[8,16,512]{2,1,0:T(8,128)} copy(f32[8,16,512]{2,1,0:T(8,128)} %get-tuple-element.4) | data formatting | bytes 524288
  57.3 0.0 copy-done
  57.3 0.7 %copy.11 = f32[8,16,512]{2,1,0:T(8,128)} copy(f32[8,16,512]{2,1,0:T(8,128)S(1)} %copy-done) | data formatting | bytes 524288
Async XLA Ops:
  55.6 1.7 %copy-start = (f32[8,16,512]{2,1,0:T(8,128)S(1)}, f32[8,16,512]{2,1,0:T(8,128)}, u32[]{:S(2)}) copy-start(f32[8,16,512]{2,1,0:T(8,128)} %get-tuple-element.5) | copy-start | bytes 786436
